TPU v7x, 32 devices: a whole 2x2x4 slice. The times are simulated.
32 devices in a mesh: grp: 4 (over y, x), ctx: 8 (over z, core).
Axes of the slice: x: 2, y: 2, z: 4, core: 2. Of those that a mesh axis runs over, the one named last changes fastest.
Arguments:
- queries: bfloat16 [4096, 1792], P(('grp', 'ctx')), may hold values from -100 to 100
- keys: bfloat16 [4096, 1792], P(('grp', 'ctx')), may hold values from -5 to 5
- values: bfloat16 [4096, 1792], P(('grp', 'ctx')), may hold values from -6 to 6
- grad_out: bfloat16 [4096, 1792], P(('grp', 'ctx')), may hold values from -6 to 6
- offsets: int32 [32], replicated, may hold values from 0 to 4096, as said below
Outputs:
- grad_queries: bfloat16 [4096, 1792], P(('grp', 'ctx'))
- grad_keys: bfloat16 [4096, 1792], P(('grp', 'ctx'))
- grad_values: bfloat16 [4096, 1792], P(('grp', 'ctx'))
Inputs may be any that keep to these rules, and one draw needn't show every extreme that they name: offsets[0] = 0 and the entries never fall; between consecutive entries below 4096 the difference is 128 to 384, one difference equals 384 exactly; after the last document that starts below 4096 every entry equals 4096, and that document ends at the slab's end.
All inputs are finite; a program needn't handle non-finite values.
Results may differ from a plain program's by a relative error of at most 0.0055.
Values may be sent and summed in bfloat16 or wider, within the bound.
A program may use at most 64 MiB of HBM per device.

v0:
```python
import jax
import jax.numpy as jnp
from jax import lax
from jax.sharding import PartitionSpec as P

HEADS = 14
HEAD_DIM = 128
MAXP = 3


NEG = -1e30


def from_behind(value, axis, by):
    peers = lax.axis_size(axis)
    pairs = [(i, i + by) for i in range(peers) if 0 <= i + by < peers]
    return lax.ppermute(value, axis, pairs)


def segments(offsets, positions, slab_len):
    found = jnp.sum((offsets[None, :] <= positions[:, None]).astype(jnp.int32), axis=1) - 1
    inside = (positions >= 0) & (positions < slab_len)
    return jnp.where(inside, found, -1)


def split_heads(block):
    return block.reshape(block.shape[0], HEADS, HEAD_DIM)


def rounded(block):
    return lax.optimization_barrier(block.astype(jnp.bfloat16)).astype(jnp.float32)


def pair_statistics(query_rows, grad_rows, row_segments, key_cols, value_cols, col_segments):
    allowed = (row_segments[:, None] == col_segments[None, :])[None]
    scores = jnp.einsum(
        "qhd,khd->hqk",
        split_heads(query_rows),
        split_heads(key_cols),
        preferred_element_type=jnp.float32,
    ) * HEAD_DIM ** (-0.5)
    scores = jnp.where(allowed, scores, NEG)
    maximum = jnp.max(scores, axis=2)
    probs = jnp.where(allowed, jnp.exp(scores - maximum[:, :, None]), 0.0)
    dprobs = jnp.einsum(
        "qhd,khd->hqk",
        split_heads(grad_rows),
        split_heads(value_cols),
        preferred_element_type=jnp.float32,
    )
    return (maximum, jnp.sum(probs, axis=2), jnp.sum(probs * dprobs, axis=2))


def merge_statistics(first, second):
    maximum = jnp.maximum(first[0], second[0])
    scale_one = jnp.exp(first[0] - maximum)
    scale_two = jnp.exp(second[0] - maximum)
    return (
        maximum,
        first[1] * scale_one + second[1] * scale_two,
        first[2] * scale_one + second[2] * scale_two,
    )


def finalize(statistics):
    return (statistics[0] + jnp.log(statistics[1]), statistics[2] / statistics[1])


def pair_gradients(
    query_rows, grad_rows, row_segments, log_total, delta_rows, key_cols, value_cols, col_segments
):
    allowed = (row_segments[:, None] == col_segments[None, :])[None]
    scale = HEAD_DIM ** (-0.5)
    scores = (
        jnp.einsum(
            "qhd,khd->hqk",
            split_heads(query_rows),
            split_heads(key_cols),
            preferred_element_type=jnp.float32,
        )
        * scale
    )
    probs = jnp.where(allowed, jnp.exp(scores - log_total[:, :, None]), 0.0)
    dprobs = jnp.einsum(
        "qhd,khd->hqk",
        split_heads(grad_rows),
        split_heads(value_cols),
        preferred_element_type=jnp.float32,
    )
    dscores = jnp.where(allowed, probs * (dprobs - delta_rows[:, :, None]), 0.0)
    probs_low = probs.astype(jnp.bfloat16)
    dscores_low = dscores.astype(jnp.bfloat16)
    length = query_rows.shape[0]
    width = query_rows.shape[1]
    grad_query = (
        jnp.einsum(
            "hqk,khd->qhd", dscores_low, split_heads(key_cols), preferred_element_type=jnp.float32
        )
        * scale
    )
    grad_key = (
        jnp.einsum(
            "hqk,qhd->khd", dscores_low, split_heads(query_rows), preferred_element_type=jnp.float32
        )
        * scale
    )
    grad_value = jnp.einsum(
        "hqk,qhd->khd", probs_low, split_heads(grad_rows), preferred_element_type=jnp.float32
    )
    return (
        grad_query.reshape(length, width),
        grad_key.reshape(length, width),
        grad_value.reshape(length, width),
    )


def guarded(compute):
    result = compute()
    return result


def on_device(queries, keys, values, grad_out, offsets):
    block_len = queries.shape[0]
    device_count = lax.axis_size(("grp", "ctx"))
    slab_len = device_count * block_len
    device_index = lax.axis_index(("grp", "ctx"))
    own_positions = device_index * block_len + jnp.arange(block_len, dtype=jnp.int32)
    own_segments = segments(offsets, own_positions, slab_len)
    row_stats = pair_statistics(queries, grad_out, own_segments, keys, values, own_segments)
    received = []
    for distance in range(1, MAXP + 1):
        far_query, far_key, far_value, far_grad = from_behind(
            (queries, keys, values, grad_out), ("grp", "ctx"), -distance
        )
        far_segments = segments(offsets, own_positions + distance * block_len, slab_len)
        shared = jnp.any(own_segments[:, None] == far_segments[None, :])
        forward_stats = guarded(
            lambda: pair_statistics(
                queries, grad_out, own_segments, far_key, far_value, far_segments
            )
        )
        reverse_stats = guarded(
            lambda: pair_statistics(far_query, far_grad, far_segments, keys, values, own_segments)
        )
        row_stats = merge_statistics(row_stats, forward_stats)
        returned = from_behind(reverse_stats, ("grp", "ctx"), distance)
        row_stats = merge_statistics(row_stats, returned)
        received.append((far_query, far_key, far_value, far_grad, far_segments, shared))
    log_total, delta_rows = finalize(row_stats)
    grad_query, grad_key, grad_value = pair_gradients(
        queries, grad_out, own_segments, log_total, delta_rows, keys, values, own_segments
    )
    for distance in range(1, MAXP + 1):
        far_query, far_key, far_value, far_grad, far_segments, shared = received[distance - 1]
        far_total, far_delta = from_behind((log_total, delta_rows), ("grp", "ctx"), -distance)
        forward_terms = guarded(
            lambda: pair_gradients(
                queries,
                grad_out,
                own_segments,
                log_total,
                delta_rows,
                far_key,
                far_value,
                far_segments,
            )
        )
        reverse_terms = guarded(
            lambda: pair_gradients(
                far_query, far_grad, far_segments, far_total, far_delta, keys, values, own_segments
            )
        )
        grad_query = grad_query + rounded(forward_terms[0])
        grad_key = grad_key + rounded(reverse_terms[1])
        grad_value = grad_value + rounded(reverse_terms[2])
        outgoing = (
            forward_terms[1].astype(jnp.bfloat16),
            forward_terms[2].astype(jnp.bfloat16),
            reverse_terms[0].astype(jnp.bfloat16),
        )
        back_key, back_value, back_query = from_behind(
            (outgoing[0], outgoing[1], outgoing[2]), ("grp", "ctx"), distance
        )
        grad_query = grad_query + back_query.astype(jnp.float32)
        grad_key = grad_key + back_key.astype(jnp.float32)
        grad_value = grad_value + back_value.astype(jnp.float32)
    return (
        grad_query.astype(jnp.bfloat16),
        grad_key.astype(jnp.bfloat16),
        grad_value.astype(jnp.bfloat16),
    )


def solution(mesh):
    placed = (
        P(("grp", "ctx"), None),
        P(("grp", "ctx"), None),
        P(("grp", "ctx"), None),
        P(("grp", "ctx"), None),
        P(),
    )
    return jax.shard_map(
        on_device,
        mesh=mesh,
        in_specs=placed,
        out_specs=(P(("grp", "ctx"), None), P(("grp", "ctx"), None), P(("grp", "ctx"), None)),
        check_vma=False,
    )
```

profile of v0, /device:TPU:4, one launch (start us, length us, event | category | flops | bytes accessed | tf_op | source)
XLA Modules:
  0.0 319.1 jit_solution(16487489285208769106)
XLA Ops:
  2.0 4.9 %collective-permute-start.7 = (bf16[128,1792]{0,1:T(8,128)(2,1)S(1)}, bf16[128,1792]{0,1:T(8,128)(2,1)S(1)}, u32[]{:S(2)}, u32[]{:S(2)}) collective-permute-start(bf16[128,1792]{0,1:T(8,128)(2,1)S(1)} %copy.173), channel_id=1, source_target_pairs={{3,0},{4,1},{5,2},{6,3},{7,4},{8,5},{9,6},{10,7},{11,8},{12,9},{13... | collective-permute-start | bytes 1376264 | tf_op jit(solution)/shard_map/ppermute | solution.py:17
  6.9 3.5 %collective-permute-start.4 = (bf16[128,1792]{0,1:T(8,128)(2,1)S(1)}, bf16[128,1792]{0,1:T(8,128)(2,1)S(1)}, u32[]{:S(2)}, u32[]{:S(2)}) collective-permute-start(bf16[128,1792]{0,1:T(8,128)(2,1)S(1)} %copy.173), channel_id=1, source_target_pairs={{2,0},{3,1},{4,2},{5,3},{6,4},{7,5},{8,6},{9,7},{10,8},{11,9},{12,... | collective-permute-start | bytes 1376264 | tf_op jit(solution)/shard_map/ppermute | solution.py:17
  12.9 3.5 %collective-permute-start.6 = (bf16[128,1792]{0,1:T(8,128)(2,1)S(1)}, bf16[128,1792]{0,1:T(8,128)(2,1)}, u32[]{:S(2)}, u32[]{:S(2)}) collective-permute-start(bf16[128,1792]{0,1:T(8,128)(2,1)S(1)} %copy.174), channel_id=1, source_target_pairs={{3,0},{4,1},{5,2},{6,3},{7,4},{8,5},{9,6},{10,7},{11,8},{12,9},{13... | collective-permute-start | bytes 1376264 | tf_op jit(solution)/shard_map/ppermute | solution.py:17
  18.4 2.3 collective-permute-start.18
  23.5 4.0 %collective-permute-start.16 = (bf16[128,1792]{0,1:T(8,128)(2,1)S(1)}, bf16[128,1792]{0,1:T(8,128)(2,1)S(1)}, u32[]{:S(2)}, u32[]{:S(2)}) collective-permute-start(bf16[128,1792]{0,1:T(8,128)(2,1)S(1)} %copy.195), channel_id=1, source_target_pairs={{2,0},{3,1},{4,2},{5,3},{6,4},{7,5},{8,6},{9,7},{10,8},{11,9},{12,... | collective-permute-start | bytes 1376264 | tf_op jit(solution)/shard_map/ppermute | solution.py:17
  28.9 7.6 %collective-permute-done.19 = bf16[128,1792]{0,1:T(8,128)(2,1)S(1)} collective-permute-done((bf16[128,1792]{0,1:T(8,128)(2,1)S(1)}, bf16[128,1792]{0,1:T(8,128)(2,1)S(1)}, u32[]{:S(2)}, u32[]{:S(2)}) %collective-permute-start.19) | collective-permute-done | bytes 458784 | tf_op jit(solution)/shard_map/ppermute | solution.py:17
  36.5 10.0 %collective-permute-start.3 = (bf16[128,1792]{0,1:T(8,128)(2,1)S(1)}, bf16[128,1792]{0,1:T(8,128)(2,1)S(1)}, u32[]{:S(2)}, u32[]{:S(2)}) collective-permute-start(bf16[128,1792]{0,1:T(8,128)(2,1)S(1)} %copy.174), channel_id=1, source_target_pairs={{2,0},{3,1},{4,2},{5,3},{6,4},{7,5},{8,6},{9,7},{10,8},{11,9},{12,... | collective-permute-start | bytes 1376264 | tf_op jit(solution)/shard_map/ppermute | solution.py:17
  46.6 2.3 fusion.25
  48.9 41.7 %collective-permute-start.15 = (bf16[128,1792]{0,1:T(8,128)(2,1)}, bf16[128,1792]{0,1:T(8,128)(2,1)S(1)}, u32[]{:S(2)}, u32[]{:S(2)}) collective-permute-start(bf16[128,1792]{0,1:T(8,128)(2,1)} %copy.196), channel_id=1, source_target_pairs={{2,0},{3,1},{4,2},{5,3},{6,4},{7,5},{8,6},{9,7},{10,8},{11,9},{12,... | collective-permute-start | bytes 1376264 | tf_op jit(solution)/shard_map/ppermute | solution.py:17
  92.0 21.8 %collective-permute-start.1 = (bf16[128,1792]{0,1:T(8,128)(2,1)S(1)}, bf16[128,1792]{0,1:T(8,128)(2,1)S(1)}, u32[]{:S(2)}, u32[]{:S(2)}) collective-permute-start(bf16[128,1792]{0,1:T(8,128)(2,1)S(1)} %copy.173), channel_id=1, source_target_pairs={{1,0},{2,1},{3,2},{4,3},{5,4},{6,5},{7,6},{8,7},{9,8},{10,9},{11,1... | collective-permute-start | bytes 1376264 | tf_op jit(solution)/shard_map/ppermute | solution.py:17
  120.6 2.3 fusion.23
  122.9 4.3 %collective-permute-start.12 = (bf16[128,1792]{0,1:T(8,128)(2,1)}, bf16[128,1792]{0,1:T(8,128)(2,1)S(1)}, u32[]{:S(2)}, u32[]{:S(2)}) collective-permute-start(bf16[128,1792]{0,1:T(8,128)(2,1)} %copy.196), channel_id=1, source_target_pairs={{1,0},{2,1},{3,2},{4,3},{5,4},{6,5},{7,6},{8,7},{9,8},{10,9},{11,1... | collective-permute-start | bytes 1376264 | tf_op jit(solution)/shard_map/ppermute | solution.py:17
  129.5 2.3 fusion.21
  142.7 2.1 collective-permute-start.5
  149.3 4.7 %collective-permute-done.10 = f32[14,128]{1,0:T(8,128)S(1)} collective-permute-done((f32[14,128]{1,0:T(8,128)S(1)}, f32[14,128]{1,0:T(8,128)S(1)}, u32[]{:S(2)}, u32[]{:S(2)}) %collective-permute-start.10) | collective-permute-done | bytes 7200 | tf_op jit(solution)/shard_map/ppermute | solution.py:17
  157.5 4.8 %collective-permute-start.25 = (f32[14,128]{1,0:T(8,128)S(1)}, f32[14,128]{1,0:T(8,128)S(1)}, u32[]{:S(2)}, u32[]{:S(2)}) collective-permute-start(f32[14,128]{1,0:T(8,128)S(1)} %add_divide_fusion), channel_id=1, source_target_pairs={{2,0},{3,1},{4,2},{5,3},{6,4},{7,5},{8,6},{9,7},{10,8},{11,9},{12,... | collective-permute-start | bytes 21512 | tf_op jit(solution)/shard_map/ppermute | solution.py:17
  162.4 7.4 %collective-permute-start.27 = (f32[14,128]{1,0:T(8,128)S(1)}, f32[14,128]{1,0:T(8,128)S(1)}, u32[]{:S(2)}, u32[]{:S(2)}) collective-permute-start(f32[14,128]{1,0:T(8,128)S(1)} %log_add_fusion), channel_id=1, source_target_pairs={{3,0},{4,1},{5,2},{6,3},{7,4},{8,5},{9,6},{10,7},{11,8},{12,9},{13... | collective-permute-start | bytes 21512 | tf_op jit(solution)/shard_map/ppermute | solution.py:17
  169.8 4.4 %collective-permute-start.24 = (f32[14,128]{1,0:T(8,128)S(1)}, f32[14,128]{1,0:T(8,128)S(1)}, u32[]{:S(2)}, u32[]{:S(2)}) collective-permute-start(f32[14,128]{1,0:T(8,128)S(1)} %log_add_fusion), channel_id=1, source_target_pairs={{2,0},{3,1},{4,2},{5,3},{6,4},{7,5},{8,6},{9,7},{10,8},{11,9},{12,... | collective-permute-start | bytes 21512 | tf_op jit(solution)/shard_map/ppermute | solution.py:17
  174.3 2.1 collective-permute-start.22
  177.5 2.1 fusion.10
  193.2 2.1 copy.228
  198.5 2.1 copy.219
  201.6 2.1 copy.240
  208.9 2.1 copy.254
  214.3 3.6 %collective-permute-start.21 = (f32[14,128]{1,0:T(8,128)S(1)}, f32[14,128]{1,0:T(8,128)S(1)}, u32[]{:S(2)}, u32[]{:S(2)}) collective-permute-start(f32[14,128]{1,0:T(8,128)S(1)} %log_add_fusion), channel_id=1, source_target_pairs={{1,0},{2,1},{3,2},{4,3},{5,4},{6,5},{7,6},{8,7},{9,8},{10,9},{11,1... | collective-permute-start | bytes 21512 | tf_op jit(solution)/shard_map/ppermute | solution.py:17
  223.6 2.4 collective-permute-start.31
  232.4 2.2 collective-permute-start.34
  251.0 28.7 %collective-permute-done.32 = bf16[128,1792]{1,0:T(8,128)(2,1)} collective-permute-done((bf16[128,1792]{1,0:T(8,128)(2,1)}, bf16[128,1792]{1,0:T(8,128)(2,1)}, u32[]{:S(2)}, u32[]{:S(2)}) %collective-permute-start.32) | collective-permute-done | bytes 458784 | tf_op jit(solution)/shard_map/ppermute | solution.py:17
  285.5 2.7 add_convert_fusion.1
  290.4 3.5 %collective-permute-done.33 = bf16[128,1792]{1,0:T(8,128)(2,1)S(1)} collective-permute-done((bf16[128,1792]{1,0:T(8,128)(2,1)}, bf16[128,1792]{1,0:T(8,128)(2,1)S(1)}, u32[]{:S(2)}, u32[]{:S(2)}) %collective-permute-start.33) | collective-permute-done | bytes 458784 | tf_op jit(solution)/shard_map/ppermute | solution.py:17
  293.9 2.3 add_convert_fusion
  296.2 21.7 %collective-permute-done.29 = bf16[128,1792]{1,0:T(8,128)(2,1)S(1)} collective-permute-done((bf16[128,1792]{1,0:T(8,128)(2,1)}, bf16[128,1792]{1,0:T(8,128)(2,1)S(1)}, u32[]{:S(2)}, u32[]{:S(2)}) %collective-permute-start.29) | collective-permute-done | bytes 458784 | tf_op jit(solution)/shard_map/ppermute | solution.py:17
  (185 shorter events, 103.7 us)
Async XLA Ops:
  2.0 21.5 %collective-permute-start.7 = (bf16[128,1792]{0,1:T(8,128)(2,1)S(1)}, bf16[128,1792]{0,1:T(8,128)(2,1)S(1)}, u32[]{:S(2)}, u32[]{:S(2)}) collective-permute-start(bf16[128,1792]{0,1:T(8,128)(2,1)S(1)} %copy.173), channel_id=1, source_target_pairs={{3,0},{4,1},{5,2},{6,3},{7,4},{8,5},{9,6},{10,7},{11,8},{12,9},{13... | collective-permute-start | bytes 1376264 | tf_op jit(solution)/shard_map/ppermute | solution.py:17
  6.9 108.4 %collective-permute-start.4 = (bf16[128,1792]{0,1:T(8,128)(2,1)S(1)}, bf16[128,1792]{0,1:T(8,128)(2,1)S(1)}, u32[]{:S(2)}, u32[]{:S(2)}) collective-permute-start(bf16[128,1792]{0,1:T(8,128)(2,1)S(1)} %copy.173), channel_id=1, source_target_pairs={{2,0},{3,1},{4,2},{5,3},{6,4},{7,5},{8,6},{9,7},{10,8},{11,9},{12,... | collective-permute-start | bytes 1376264 | tf_op jit(solution)/shard_map/ppermute | solution.py:17
  10.7 25.8 %collective-permute-start.19 = (bf16[128,1792]{0,1:T(8,128)(2,1)S(1)}, bf16[128,1792]{0,1:T(8,128)(2,1)S(1)}, u32[]{:S(2)}, u32[]{:S(2)}) collective-permute-start(bf16[128,1792]{0,1:T(8,128)(2,1)S(1)} %copy.195), channel_id=1, source_target_pairs={{3,0},{4,1},{5,2},{6,3},{7,4},{8,5},{9,6},{10,7},{11,8},{12,9},{13... | collective-permute-start | bytes 1376264 | tf_op jit(solution)/shard_map/ppermute | solution.py:17
  12.9 36.0 %collective-permute-start.6 = (bf16[128,1792]{0,1:T(8,128)(2,1)S(1)}, bf16[128,1792]{0,1:T(8,128)(2,1)}, u32[]{:S(2)}, u32[]{:S(2)}) collective-permute-start(bf16[128,1792]{0,1:T(8,128)(2,1)S(1)} %copy.174), channel_id=1, source_target_pairs={{3,0},{4,1},{5,2},{6,3},{7,4},{8,5},{9,6},{10,7},{11,8},{12,9},{13... | collective-permute-start | bytes 1376264 | tf_op jit(solution)/shard_map/ppermute | solution.py:17
  18.4 73.6 %collective-permute-start.18 = (bf16[128,1792]{0,1:T(8,128)(2,1)}, bf16[128,1792]{0,1:T(8,128)(2,1)}, u32[]{:S(2)}, u32[]{:S(2)}) collective-permute-start(bf16[128,1792]{0,1:T(8,128)(2,1)} %copy.196), channel_id=1, source_target_pairs={{3,0},{4,1},{5,2},{6,3},{7,4},{8,5},{9,6},{10,7},{11,8},{12,9},{13... | collective-permute-start | bytes 1376264 | tf_op jit(solution)/shard_map/ppermute | solution.py:17
  23.5 95.1 %collective-permute-start.16 = (bf16[128,1792]{0,1:T(8,128)(2,1)S(1)}, bf16[128,1792]{0,1:T(8,128)(2,1)S(1)}, u32[]{:S(2)}, u32[]{:S(2)}) collective-permute-start(bf16[128,1792]{0,1:T(8,128)(2,1)S(1)} %copy.195), channel_id=1, source_target_pairs={{2,0},{3,1},{4,2},{5,3},{6,4},{7,5},{8,6},{9,7},{10,8},{11,9},{12,... | collective-permute-start | bytes 1376264 | tf_op jit(solution)/shard_map/ppermute | solution.py:17
  36.5 95.3 %collective-permute-start.3 = (bf16[128,1792]{0,1:T(8,128)(2,1)S(1)}, bf16[128,1792]{0,1:T(8,128)(2,1)S(1)}, u32[]{:S(2)}, u32[]{:S(2)}) collective-permute-start(bf16[128,1792]{0,1:T(8,128)(2,1)S(1)} %copy.174), channel_id=1, source_target_pairs={{2,0},{3,1},{4,2},{5,3},{6,4},{7,5},{8,6},{9,7},{10,8},{11,9},{12,... | collective-permute-start | bytes 1376264 | tf_op jit(solution)/shard_map/ppermute | solution.py:17
  48.9 85.3 %collective-permute-start.15 = (bf16[128,1792]{0,1:T(8,128)(2,1)}, bf16[128,1792]{0,1:T(8,128)(2,1)S(1)}, u32[]{:S(2)}, u32[]{:S(2)}) collective-permute-start(bf16[128,1792]{0,1:T(8,128)(2,1)} %copy.196), channel_id=1, source_target_pairs={{2,0},{3,1},{4,2},{5,3},{6,4},{7,5},{8,6},{9,7},{10,8},{11,9},{12,... | collective-permute-start | bytes 1376264 | tf_op jit(solution)/shard_map/ppermute | solution.py:17
  92.0 30.9 %collective-permute-start.1 = (bf16[128,1792]{0,1:T(8,128)(2,1)S(1)}, bf16[128,1792]{0,1:T(8,128)(2,1)S(1)}, u32[]{:S(2)}, u32[]{:S(2)}) collective-permute-start(bf16[128,1792]{0,1:T(8,128)(2,1)S(1)} %copy.173), channel_id=1, source_target_pairs={{1,0},{2,1},{3,2},{4,3},{5,4},{6,5},{7,6},{8,7},{9,8},{10,9},{11,1... | collective-permute-start | bytes 1376264 | tf_op jit(solution)/shard_map/ppermute | solution.py:17
  115.3 12.3 %collective-permute-start.13 = (bf16[128,1792]{0,1:T(8,128)(2,1)S(1)}, bf16[128,1792]{0,1:T(8,128)(2,1)S(1)}, u32[]{:S(2)}, u32[]{:S(2)}) collective-permute-start(bf16[128,1792]{0,1:T(8,128)(2,1)S(1)} %copy.195), channel_id=1, source_target_pairs={{1,0},{2,1},{3,2},{4,3},{5,4},{6,5},{7,6},{8,7},{9,8},{10,9},{11,1... | collective-permute-start | bytes 1376264 | tf_op jit(solution)/shard_map/ppermute | solution.py:17
  118.6 17.9 %collective-permute-start = (bf16[128,1792]{0,1:T(8,128)(2,1)S(1)}, bf16[128,1792]{0,1:T(8,128)(2,1)S(1)}, u32[]{:S(2)}, u32[]{:S(2)}) collective-permute-start(bf16[128,1792]{0,1:T(8,128)(2,1)S(1)} %copy.174), channel_id=1, source_target_pairs={{1,0},{2,1},{3,2},{4,3},{5,4},{6,5},{7,6},{8,7},{9,8},{10,9},{11,1... | collective-permute-start | bytes 1376264 | tf_op jit(solution)/shard_map/ppermute | solution.py:17
  122.9 15.9 %collective-permute-start.12 = (bf16[128,1792]{0,1:T(8,128)(2,1)}, bf16[128,1792]{0,1:T(8,128)(2,1)S(1)}, u32[]{:S(2)}, u32[]{:S(2)}) collective-permute-start(bf16[128,1792]{0,1:T(8,128)(2,1)} %copy.196), channel_id=1, source_target_pairs={{1,0},{2,1},{3,2},{4,3},{5,4},{6,5},{7,6},{8,7},{9,8},{10,9},{11,1... | collective-permute-start | bytes 1376264 | tf_op jit(solution)/shard_map/ppermute | solution.py:17
  127.6 13.2 %collective-permute-start.20 = (f32[14,128]{1,0:T(8,128)S(1)}, f32[14,128]{1,0:T(8,128)S(1)}, u32[]{:S(2)}, u32[]{:S(2)}) collective-permute-start(f32[14,128]{1,0:T(8,128)S(1)} %get-tuple-element.16), channel_id=1, source_target_pairs={{0,3},{1,4},{2,5},{3,6},{4,7},{5,8},{6,9},{7,10},{8,11},{9,12},{10... | collective-permute-start | bytes 21512 | tf_op jit(solution)/shard_map/ppermute | solution.py:17
  131.8 10.8 %collective-permute-start.17 = (f32[14,128]{1,0:T(8,128)S(1)}, f32[14,128]{1,0:T(8,128)S(1)}, u32[]{:S(2)}, u32[]{:S(2)}) collective-permute-start(f32[14,128]{1,0:T(8,128)S(1)} %get-tuple-element.12), channel_id=1, source_target_pairs={{0,2},{1,3},{2,4},{3,5},{4,6},{5,7},{6,8},{7,9},{8,10},{9,11},{10,... | collective-permute-start | bytes 21512 | tf_op jit(solution)/shard_map/ppermute | solution.py:17
  134.1 10.7 %collective-permute-start.14 = (f32[14,128]{1,0:T(8,128)S(1)}, f32[14,128]{1,0:T(8,128)S(1)}, u32[]{:S(2)}, u32[]{:S(2)}) collective-permute-start(f32[14,128]{1,0:T(8,128)S(1)} %get-tuple-element.8), channel_id=1, source_target_pairs={{0,1},{1,2},{2,3},{3,4},{4,5},{5,6},{6,7},{7,8},{8,9},{9,10},{10,1... | collective-permute-start | bytes 21512 | tf_op jit(solution)/shard_map/ppermute | solution.py:17
  138.8 10.5 %collective-permute-start.8 = (f32[14,128]{1,0:T(8,128)S(1)}, f32[14,128]{1,0:T(8,128)S(1)}, u32[]{:S(2)}, u32[]{:S(2)}) collective-permute-start(f32[14,128]{1,0:T(8,128)S(1)} %get-tuple-element.36), channel_id=1, source_target_pairs={{0,3},{1,4},{2,5},{3,6},{4,7},{5,8},{6,9},{7,10},{8,11},{9,12},{10... | collective-permute-start | bytes 21512 | tf_op jit(solution)/shard_map/ppermute | solution.py:17
  142.7 12.7 %collective-permute-start.5 = (f32[14,128]{1,0:T(8,128)S(1)}, f32[14,128]{1,0:T(8,128)S(1)}, u32[]{:S(2)}, u32[]{:S(2)}) collective-permute-start(f32[14,128]{1,0:T(8,128)S(1)} %get-tuple-element.42), channel_id=1, source_target_pairs={{0,2},{1,3},{2,4},{3,5},{4,6},{5,7},{6,8},{7,9},{8,10},{9,11},{10,... | collective-permute-start | bytes 21512 | tf_op jit(solution)/shard_map/ppermute | solution.py:17
  155.4 58.9 %collective-permute-start.28 = (f32[14,128]{1,0:T(8,128)S(1)}, f32[14,128]{1,0:T(8,128)S(1)}, u32[]{:S(2)}, u32[]{:S(2)}) collective-permute-start(f32[14,128]{1,0:T(8,128)S(1)} %add_divide_fusion), channel_id=1, source_target_pairs={{3,0},{4,1},{5,2},{6,3},{7,4},{8,5},{9,6},{10,7},{11,8},{12,9},{13... | collective-permute-start | bytes 21512 | tf_op jit(solution)/shard_map/ppermute | solution.py:17
  157.5 66.1 %collective-permute-start.25 = (f32[14,128]{1,0:T(8,128)S(1)}, f32[14,128]{1,0:T(8,128)S(1)}, u32[]{:S(2)}, u32[]{:S(2)}) collective-permute-start(f32[14,128]{1,0:T(8,128)S(1)} %add_divide_fusion), channel_id=1, source_target_pairs={{2,0},{3,1},{4,2},{5,3},{6,4},{7,5},{8,6},{9,7},{10,8},{11,9},{12,... | collective-permute-start | bytes 21512 | tf_op jit(solution)/shard_map/ppermute | solution.py:17
  162.4 55.5 %collective-permute-start.27 = (f32[14,128]{1,0:T(8,128)S(1)}, f32[14,128]{1,0:T(8,128)S(1)}, u32[]{:S(2)}, u32[]{:S(2)}) collective-permute-start(f32[14,128]{1,0:T(8,128)S(1)} %log_add_fusion), channel_id=1, source_target_pairs={{3,0},{4,1},{5,2},{6,3},{7,4},{8,5},{9,6},{10,7},{11,8},{12,9},{13... | collective-permute-start | bytes 21512 | tf_op jit(solution)/shard_map/ppermute | solution.py:17
  169.8 56.1 %collective-permute-start.24 = (f32[14,128]{1,0:T(8,128)S(1)}, f32[14,128]{1,0:T(8,128)S(1)}, u32[]{:S(2)}, u32[]{:S(2)}) collective-permute-start(f32[14,128]{1,0:T(8,128)S(1)} %log_add_fusion), channel_id=1, source_target_pairs={{2,0},{3,1},{4,2},{5,3},{6,4},{7,5},{8,6},{9,7},{10,8},{11,9},{12,... | collective-permute-start | bytes 21512 | tf_op jit(solution)/shard_map/ppermute | solution.py:17
  174.3 56.2 %collective-permute-start.22 = (f32[14,128]{1,0:T(8,128)S(1)}, f32[14,128]{1,0:T(8,128)S(1)}, u32[]{:S(2)}, u32[]{:S(2)}) collective-permute-start(f32[14,128]{1,0:T(8,128)S(1)} %add_divide_fusion), channel_id=1, source_target_pairs={{1,0},{2,1},{3,2},{4,3},{5,4},{6,5},{7,6},{8,7},{9,8},{10,9},{11,1... | collective-permute-start | bytes 21512 | tf_op jit(solution)/shard_map/ppermute | solution.py:17
  214.3 18.1 %collective-permute-start.21 = (f32[14,128]{1,0:T(8,128)S(1)}, f32[14,128]{1,0:T(8,128)S(1)}, u32[]{:S(2)}, u32[]{:S(2)}) collective-permute-start(f32[14,128]{1,0:T(8,128)S(1)} %log_add_fusion), channel_id=1, source_target_pairs={{1,0},{2,1},{3,2},{4,3},{5,4},{6,5},{7,6},{8,7},{9,8},{10,9},{11,1... | collective-permute-start | bytes 21512 | tf_op jit(solution)/shard_map/ppermute | solution.py:17
  217.9 61.9 %collective-permute-start.32 = (bf16[128,1792]{1,0:T(8,128)(2,1)}, bf16[128,1792]{1,0:T(8,128)(2,1)}, u32[]{:S(2)}, u32[]{:S(2)}) collective-permute-start(bf16[128,1792]{1,0:T(8,128)(2,1)} %copy.244), channel_id=1, source_target_pairs={{0,3},{1,4},{2,5},{3,6},{4,7},{5,8},{6,9},{7,10},{8,11},{9,12},{10... | collective-permute-start | bytes 1376264 | tf_op jit(solution)/shard_map/ppermute | solution.py:17
  223.6 58.1 %collective-permute-start.31 = (bf16[128,1792]{1,0:T(8,128)(2,1)}, bf16[128,1792]{1,0:T(8,128)(2,1)}, u32[]{:S(2)}, u32[]{:S(2)}) collective-permute-start(bf16[128,1792]{1,0:T(8,128)(2,1)} %copy.240), channel_id=1, source_target_pairs={{0,2},{1,3},{2,4},{3,5},{4,6},{5,7},{6,8},{7,9},{8,10},{9,11},{10,... | collective-permute-start | bytes 1376264 | tf_op jit(solution)/shard_map/ppermute | solution.py:17
  226.0 57.6 %collective-permute-start.30 = (bf16[128,1792]{1,0:T(8,128)(2,1)}, bf16[128,1792]{1,0:T(8,128)(2,1)}, u32[]{:S(2)}, u32[]{:S(2)}) collective-permute-start(bf16[128,1792]{1,0:T(8,128)(2,1)} %copy.236), channel_id=1, source_target_pairs={{0,1},{1,2},{2,3},{3,4},{4,5},{5,6},{6,7},{7,8},{8,9},{9,10},{10,1... | collective-permute-start | bytes 1376264 | tf_op jit(solution)/shard_map/ppermute | solution.py:17
  230.5 57.8 %collective-permute-start.35 = (bf16[128,1792]{1,0:T(8,128)(2,1)}, bf16[128,1792]{1,0:T(8,128)(2,1)}, u32[]{:S(2)}, u32[]{:S(2)}) collective-permute-start(bf16[128,1792]{1,0:T(8,128)(2,1)} %copy.258), channel_id=1, source_target_pairs={{0,3},{1,4},{2,5},{3,6},{4,7},{5,8},{6,9},{7,10},{8,11},{9,12},{10... | collective-permute-start | bytes 1376264 | tf_op jit(solution)/shard_map/ppermute | solution.py:17
  232.4 58.0 %collective-permute-start.34 = (bf16[128,1792]{1,0:T(8,128)(2,1)}, bf16[128,1792]{1,0:T(8,128)(2,1)}, u32[]{:S(2)}, u32[]{:S(2)}) collective-permute-start(bf16[128,1792]{1,0:T(8,128)(2,1)} %copy.254), channel_id=1, source_target_pairs={{0,2},{1,3},{2,4},{3,5},{4,6},{5,7},{6,8},{7,9},{8,10},{9,11},{10,... | collective-permute-start | bytes 1376264 | tf_op jit(solution)/shard_map/ppermute | solution.py:17
  279.7 14.1 %collective-permute-start.33 = (bf16[128,1792]{1,0:T(8,128)(2,1)}, bf16[128,1792]{1,0:T(8,128)(2,1)S(1)}, u32[]{:S(2)}, u32[]{:S(2)}) collective-permute-start(bf16[128,1792]{1,0:T(8,128)(2,1)} %copy.250), channel_id=1, source_target_pairs={{0,1},{1,2},{2,3},{3,4},{4,5},{5,6},{6,7},{7,8},{8,9},{9,10},{10,1... | collective-permute-start | bytes 1376264 | tf_op jit(solution)/shard_map/ppermute | solution.py:17
  281.7 36.2 %collective-permute-start.29 = (bf16[128,1792]{1,0:T(8,128)(2,1)}, bf16[128,1792]{1,0:T(8,128)(2,1)S(1)}, u32[]{:S(2)}, u32[]{:S(2)}) collective-permute-start(bf16[128,1792]{1,0:T(8,128)(2,1)} %copy.230), channel_id=1, source_target_pairs={{0,3},{1,4},{2,5},{3,6},{4,7},{5,8},{6,9},{7,10},{8,11},{9,12},{10... | collective-permute-start | bytes 1376264 | tf_op jit(solution)/shard_map/ppermute | solution.py:17
  283.6 34.3 %collective-permute-start.26 = (bf16[128,1792]{1,0:T(8,128)(2,1)}, bf16[128,1792]{1,0:T(8,128)(2,1)S(1)}, u32[]{:S(2)}, u32[]{:S(2)}) collective-permute-start(bf16[128,1792]{1,0:T(8,128)(2,1)} %copy.226), channel_id=1, source_target_pairs={{0,2},{1,3},{2,4},{3,5},{4,6},{5,7},{6,8},{7,9},{8,10},{9,11},{10,... | collective-permute-start | bytes 1376264 | tf_op jit(solution)/shard_map/ppermute | solution.py:17
  288.3 29.6 %collective-permute-start.23 = (bf16[128,1792]{1,0:T(8,128)(2,1)S(1)}, bf16[128,1792]{1,0:T(8,128)(2,1)S(1)}, u32[]{:S(2)}, u32[]{:S(2)}) collective-permute-start(bf16[128,1792]{1,0:T(8,128)(2,1)S(1)} %copy-done.32), channel_id=1, source_target_pairs={{0,1},{1,2},{2,3},{3,4},{4,5},{5,6},{6,7},{7,8},{8,9},{9,10},{10,1... | collective-permute-start | bytes 1376264 | tf_op jit(solution)/shard_map/ppermute | solution.py:17
  (38 other events, 447.4 us)
where the time goes:
time: 321 us; the launch traced here: 319 us
  starting transfers between devices  162 us (50%)
  waiting for transfers between devices  67.7 us (21%)
  matrix products  41.2 us (13%)
  local copies, waits for them, and re-layouts  37 us (12%)
  other arithmetic  9.65 us (3%)
    ppermute x36, starting transfers between devices, from_behind(): return lax.ppermute(value, axis, pairs)  162 us
    ppermute x36, waiting for transfers between devices, from_behind(): return lax.ppermute(value, axis, pairs)  67.7 us
    optimization_barrier x9, local copies, waits for them, and re-layouts, rounded(): lax.optimization_barrier(block.astype(jnp.bfloat16)).astype(jnp.float32)  11.7 us
    dot_general x6, matrix products, pair_statistics(): jnp.einsum('qhd,khd->hqk', split_heads(grad_rows), split_heads(value_cols...  9.32 us
    dot_general x7, matrix products, pair_gradients(): jnp.einsum('hqk,qhd->khd', dscores_low, split_heads(query_rows), preferre...  8.85 us
    dot_general x7, matrix products, pair_gradients(): jnp.einsum('hqk,khd->qhd', dscores_low, split_heads(key_cols), preferred_...  8.57 us
    dot_general x7, matrix products, pair_gradients(): jnp.einsum('hqk,qhd->khd', probs_low, split_heads(grad_rows), preferred_e...  7.53 us
  transfers between devices with their start and end apart: 36, of which 6 were waited for; matrix products, arithmetic and copies ran while one was open for 26% of the time, Pallas kernels for 0%

commit v1 on v0

v1 whole, which is shorter than its diff:
```python
import functools
import math

import jax
import jax.numpy as jnp
from jax import lax
from jax.experimental import pallas as pl
from jax.experimental.pallas import tpu as pltpu
from jax.sharding import PartitionSpec as P

HEAD_DIM = 128
NEG = -1e30
CHUNKS = 2
LOG2E = math.log2(math.e)
MESH = pl.DeviceIdType.MESH

K, V, Q, G = 0, 1, 2, 3
OWN, LOW, HIGH, MATE, MATE_LOW, MATE_HIGH, FAR = range(7)


def nt(a, b):
    return lax.dot_general(a, b, (((1,), (1,)), ((), ())), preferred_element_type=jnp.float32)


def nn(a, b):
    return lax.dot_general(a, b, (((1,), (0,)), ((), ())), preferred_element_type=jnp.float32)


def kernel(groups, inner, q_ref, k_ref, v_ref, g_ref, ofs_ref, gq_ref, gk_ref, gv_ref,
           buf, bias, stat, send_sem, recv_sem, loc_sem, ssend, srecv):
    rows, width = q_ref.shape
    heads = width // HEAD_DIM
    devices = groups * inner
    me = lax.axis_index("grp") * inner + lax.axis_index("ctx")
    core = lax.rem(me, 2)
    side = 2 * core - 1
    mate = me - side
    scale = HEAD_DIM ** -0.5

    def device(index):
        wrapped = lax.rem(index + devices, devices)
        return (lax.div(wrapped, inner), lax.rem(wrapped, inner))

    refs = [k_ref, v_ref, q_ref, g_ref]
    chunk_width = (heads // CHUNKS) * HEAD_DIM

    def cols(c):
        return pl.ds(c * chunk_width, chunk_width)

    def send(array, c, source, place, target):
        piece = array * CHUNKS + c
        src = refs[array].at[:, cols(c)] if source is None else buf.at[array, source, :, cols(c)]
        return pltpu.make_async_remote_copy(
            src_ref=src,
            dst_ref=buf.at[array, place, :, cols(c)],
            send_sem=send_sem.at[place, piece],
            recv_sem=recv_sem.at[place, piece],
            device_id=device(target),
            device_id_type=MESH,
        )

    def routes(array, c):
        return {
            LOW: send(array, c, None, LOW, me + 2),
            HIGH: send(array, c, None, HIGH, me - 2),
            MATE: send(array, c, None, MATE, mate),
            MATE_LOW: send(array, c, LOW, MATE_LOW, mate),
            MATE_HIGH: send(array, c, HIGH, MATE_HIGH, mate),
        }

    def start_own(array, c):
        r = routes(array, c)
        r[LOW].start()
        r[HIGH].start()
        r[MATE].start()

    def far_copy(array, c, source):
        return send(array, c, source, FAR, me + side)

    def forward(array, c):
        r = routes(array, c)
        r[LOW].wait_recv()

        @pl.when(core == 1)
        def _():
            far_copy(array, c, LOW).start()

        r[MATE_LOW].start()
        r[HIGH].wait_recv()

        @pl.when(core == 0)
        def _():
            far_copy(array, c, HIGH).start()

        r[MATE_HIGH].start()

    def wait_gathered(array, c):
        r = routes(array, c)
        r[MATE].wait_recv()
        r[MATE_LOW].wait_recv()
        r[MATE_HIGH].wait_recv()
        far_copy(array, c, LOW).wait_recv()

    def wait_sent(array, c):
        r = routes(array, c)
        for place in (LOW, HIGH, MATE, MATE_LOW, MATE_HIGH):
            r[place].wait_send()
        far_copy(array, c, LOW).wait_send()

    locals_ = [pltpu.make_async_copy(refs[a], buf.at[a, OWN], loc_sem.at[a]) for a in range(4)]
    for copy in locals_:
        copy.start()

    barrier = pltpu.get_barrier_semaphore()
    for distance in (-3, -2, -1, 1, 2, 3):
        pl.semaphore_signal(barrier, inc=1, device_id=device(me + distance), device_id_type=MESH)
    pl.semaphore_wait(barrier, 6)

    order = [(K, c) for c in range(0)]
    for c in range(CHUNKS):
        order += [(K, c), (V, c)]
    for c in range(CHUNKS):
        order += [(Q, c), (G, c)]
    for array, c in order:
        start_own(array, c)

    places = [me, me - 2, me + 2, mate, mate - 2, mate + 2, me + 3 * side]
    lane = lax.broadcasted_iota(jnp.int32, (1, rows), 1)
    across = jnp.concatenate([index * rows + lane for index in places], axis=1)
    down = me * rows + lax.broadcasted_iota(jnp.int32, (rows, 1), 0)

    def count(i, found):
        first = ofs_ref[i]
        return (found[0] + (first <= down).astype(jnp.int32),
                found[1] + (first <= across).astype(jnp.int32))

    seg_down, seg_across = lax.fori_loop(
        0, ofs_ref.shape[0], count, (jnp.full(down.shape, -1, jnp.int32), jnp.full(across.shape, -1, jnp.int32)))
    inside = (across >= 0) & (across < devices * rows)
    seg_across = jnp.where(inside, seg_across, -1)
    bias[...] = jnp.where(seg_down == seg_across, 0.0, NEG)

    for copy in locals_:
        copy.wait()

    def whole(array, col):
        return buf[array, :, :, col].reshape(7 * rows, HEAD_DIM)

    def head_col(h):
        return pl.ds(pl.multiple_of(h * HEAD_DIM, HEAD_DIM), HEAD_DIM)

    stat_lane = lax.broadcasted_iota(jnp.int32, (rows, HEAD_DIM), 1)

    def first_pass(h, totals):
        col = head_col(h)
        keys = whole(K, col)
        x = nt(buf[Q, OWN, :, col], keys) * (scale * LOG2E) + bias[...]
        top = jnp.max(x, axis=1, keepdims=True)
        e = jnp.exp2(x - top)
        norm = jnp.sum(e, axis=1, keepdims=True)
        dp = nt(buf[G, OWN, :, col], whole(V, col))
        inv = 1.0 / norm
        delta = jnp.sum(e * dp, axis=1, keepdims=True) * inv
        ds = ((e * inv) * (dp - delta)).astype(jnp.bfloat16)
        gq_ref[:, col] = (nn(ds, keys) * scale).astype(jnp.bfloat16)
        total = top + jnp.log(norm) * LOG2E
        return (jnp.where(stat_lane == h, total, totals[0]), jnp.where(stat_lane == h, delta, totals[1]))

    stat_rows = stat.shape[2]
    for c in range(CHUNKS):
        forward(K, c)
        forward(V, c)
    totals = (jnp.zeros((rows, HEAD_DIM), jnp.float32), jnp.zeros((rows, HEAD_DIM), jnp.float32))
    per = heads // CHUNKS
    for c in range(CHUNKS):
        wait_gathered(K, c)
        wait_gathered(V, c)
        totals = lax.fori_loop(c * per, (c + 1) * per, first_pass, totals)
    stat[0, 0] = totals[0].T[:stat_rows]
    stat[0, 1] = totals[1].T[:stat_rows]

    def slot(distance):
        return distance + 4 if distance < 0 else distance + 3

    stat_copies = [
        pltpu.make_async_remote_copy(
            src_ref=stat.at[0],
            dst_ref=stat.at[slot(-distance)],
            send_sem=ssend.at[slot(-distance)],
            recv_sem=srecv.at[slot(-distance)],
            device_id=device(me + distance),
            device_id_type=MESH,
        )
        for distance in (-3, -2, -1, 1, 2, 3)
    ]
    for copy in stat_copies:
        copy.start()

    for c in range(CHUNKS):
        forward(Q, c)
        forward(G, c)
    for copy in stat_copies:
        copy.wait_recv()

    by_place = [0, 2, 5, 4 - core, 3 - 2 * core, 6 - 2 * core, 1 + 5 * core]

    def second_pass(h, carry):
        col = head_col(h)
        queries, grads = whole(Q, col), whole(G, col)
        total = jnp.concatenate([stat[s, 0, pl.ds(h, 1), :] for s in by_place], axis=1)
        delta = jnp.concatenate([stat[s, 1, pl.ds(h, 1), :] for s in by_place], axis=1)
        x = nt(buf[K, OWN, :, col], queries) * (scale * LOG2E) + bias[...]
        p = jnp.exp2(x - total)
        dp = nt(buf[V, OWN, :, col], grads)
        ds = (p * (dp - delta)).astype(jnp.bfloat16)
        gv_ref[:, col] = nn(p.astype(jnp.bfloat16), grads).astype(jnp.bfloat16)
        gk_ref[:, col] = (nn(ds, queries) * scale).astype(jnp.bfloat16)
        return carry

    for c in range(CHUNKS):
        wait_gathered(Q, c)
        wait_gathered(G, c)
        lax.fori_loop(c * per, (c + 1) * per, second_pass, 0)

    for array, c in order:
        wait_sent(array, c)
    for copy in stat_copies:
        copy.wait_send()


def solution(mesh):
    groups, inner = mesh.shape["grp"], mesh.shape["ctx"]

    def on_device(queries, keys, values, grad_out, offsets):
        rows, width = queries.shape
        heads = width // HEAD_DIM
        stat_rows = -(-heads // 8) * 8
        block = jax.ShapeDtypeStruct((rows, width), jnp.bfloat16)
        pieces = 4 * CHUNKS
        return pl.pallas_call(
            functools.partial(kernel, groups, inner),
            out_shape=(block, block, block),
            in_specs=[pl.BlockSpec(memory_space=pl.ANY)] * 4 + [pl.BlockSpec(memory_space=pltpu.SMEM)],
            out_specs=[pl.BlockSpec(memory_space=pltpu.VMEM)] * 3,
            scratch_shapes=[
                pltpu.VMEM((4, 7, rows, width), jnp.bfloat16),
                pltpu.VMEM((rows, 7 * rows), jnp.float32),
                pltpu.VMEM((7, 2, stat_rows, rows), jnp.float32),
                pltpu.SemaphoreType.DMA((7, pieces)),
                pltpu.SemaphoreType.DMA((7, pieces)),
                pltpu.SemaphoreType.DMA((4,)),
                pltpu.SemaphoreType.DMA((7,)),
                pltpu.SemaphoreType.DMA((7,)),
            ],
            compiler_params=pltpu.CompilerParams(
                collective_id=0, has_side_effects=True, vmem_limit_bytes=48 * 1024 * 1024
            ),
        )(queries, keys, values, grad_out, offsets)

    split = P(("grp", "ctx"), None)
    return jax.shard_map(
        on_device,
        mesh=mesh,
        in_specs=(split, split, split, split, P()),
        out_specs=(split, split, split),
        check_vma=False,
    )
```

time: 321 us -> 148 us (0.46)
  the two profiles are of different devices: /device:TPU:4 before, /device:TPU:29 now
where the time goes in v1:
time: 148 us; the launch traced here: 145 us
  Pallas kernels  137 us (93%)
  local copies, waits for them, and re-layouts  7.02 us (5%)
    pallas_call x1, Pallas kernels, on_device(): pl.pallas_call(functools.partial(kernel, groups, inner), out_shape=(block...  137 us
    unnamed x13, local copies, waits for them, and re-layouts  7.02 us

profile of v1, /device:TPU:29, one launch (start us, length us, event | category | flops | bytes accessed | tf_op | source)
XLA Modules:
  0.0 145.0 jit_solution(443795725448105940)
XLA Ops:
  0.6 0.0 copy-start
  0.6 1.0 copy-done
  1.7 0.0 copy-start.1
  1.7 1.0 copy-done.1
  2.7 0.0 copy-start.2
  2.7 1.0 copy-done.2
  3.7 0.0 copy-start.3
  3.7 1.0 copy-done.3
  4.7 0.0 copy-start.4
  4.7 0.7 copy-done.4
  5.4 137.3 %shard_map.76 = (bf16[128,1792]{1,0:T(8,128)(2,1)S(1)}, bf16[128,1792]{1,0:T(8,128)(2,1)S(1)}, bf16[128,1792]{1,0:T(8,128)(2,1)S(1)}) custom-call(bf16[128,1792]{1,0:T(8,128)(2,1)S(1)} %copy-done, bf16[128,1792]{1,0:T(8,128)(2,1)S(1)} %copy-done.1, bf16[128,1792]{1,0:T(8,128)(2,1)S(1)} %copy-done.2, bf16[128,1792]{1,0:T(8,128)(2,1)S(1)} %copy-done.3, ...), custom_call_target="tpu_custom_call" | custom-call | tf_op jit(solution)/shard_map/pallas_call | solution.py:240
  142.7 0.8 copy.11
  143.5 0.8 copy.12
  144.2 0.8 copy.13
Async XLA Ops:
  0.6 1.0 copy-start
  1.7 1.0 copy-start.1
  2.7 1.0 copy-start.2
  3.7 1.0 copy-start.3
  4.7 0.7 copy-start.4

commit v2 on v1

--- a/solution.py
+++ b/solution.py
@@ -11,6 +11,8 @@
 HEAD_DIM = 128
 NEG = -1e30
 CHUNKS = 2
+RELAYED = ((0, 0), (1, 0), (0, 1))
+UPWARD_AT_FIRST = False
 LOG2E = math.log2(math.e)
 MESH = pl.DeviceIdType.MESH
 
@@ -27,7 +29,7 @@
 
 
 def kernel(groups, inner, q_ref, k_ref, v_ref, g_ref, ofs_ref, gq_ref, gk_ref, gv_ref,
-           buf, bias, stat, send_sem, recv_sem, loc_sem, ssend, srecv):
+           buf, bias, stat, held, send_sem, recv_sem, loc_sem, ssend, srecv, hsend, hrecv):
     rows, width = q_ref.shape
     heads = width // HEAD_DIM
     devices = groups * inner
@@ -35,6 +37,17 @@
     core = lax.rem(me, 2)
     side = 2 * core - 1
     mate = me - side
+    chip, chips = lax.div(me, 2), devices // 2
+    has_low, has_high = chip >= 1, chip < chips - 1
+    has_far = jnp.where(core == 0, chip >= 2, chip < chips - 2)
+    gives_far = has_low & has_high
+    grp = lax.axis_index("grp")
+    place_in_grp = lax.div(lax.axis_index("ctx"), 2)
+    per_grp = inner // 2
+    opens = (place_in_grp == 0) & (grp > 0)
+    closes = (place_in_grp == per_grp - 1) & (grp < groups - 1)
+    first, last = core, devices - 2 + core
+    up_relay, down_relay = (first, last) if UPWARD_AT_FIRST else (last, first)
     scale = HEAD_DIM ** -0.5
 
     def device(index):
@@ -59,53 +72,107 @@
             device_id_type=MESH,
         )
 
-    def routes(array, c):
-        return {
-            LOW: send(array, c, None, LOW, me + 2),
-            HIGH: send(array, c, None, HIGH, me - 2),
-            MATE: send(array, c, None, MATE, mate),
-            MATE_LOW: send(array, c, LOW, MATE_LOW, mate),
-            MATE_HIGH: send(array, c, HIGH, MATE_HIGH, mate),
-        }
-
-    def start_own(array, c):
-        r = routes(array, c)
-        r[LOW].start()
-        r[HIGH].start()
-        r[MATE].start()
+    steps = {
+        LOW: (me + 2, None, has_high, has_low),
+        HIGH: (me - 2, None, has_low, has_high),
+        MATE: (mate, None, None, None),
+        MATE_LOW: (mate, LOW, has_low, has_low),
+        MATE_HIGH: (mate, HIGH, has_high, has_high),
+    }
+
+    def where(condition, action):
+        if condition is None:
+            action()
+        else:
+            pl.when(condition)(action)
+
+    def step(array, c, place):
+        target, source, _, _ = steps[place]
+        return send(array, c, source, place, target)
 
     def far_copy(array, c, source):
         return send(array, c, source, FAR, me + side)
 
+    def start(array, c, place):
+        where(steps[place][2], lambda: step(array, c, place).start())
+
+    def wait_recv(array, c, place):
+        where(steps[place][3], lambda: step(array, c, place).wait_recv())
+
+    def to_relay(array, c, place):
+        piece = RELAYED.index((array, c))
+        boundary = grp if place == LOW else grp - 1
+        return pltpu.make_async_remote_copy(
+            src_ref=refs[array].at[:, cols(c)],
+            dst_ref=held.at[boundary, piece],
+            send_sem=send_sem.at[place, array * CHUNKS + c],
+            recv_sem=hrecv.at[boundary, piece],
+            device_id=device(up_relay if place == LOW else down_relay),
+            device_id_type=MESH,
+        )
+
+    def from_relay(array, c, place, boundary):
+        piece = RELAYED.index((array, c))
+        target = (boundary + 1) * inner + core if place == LOW else boundary * inner + inner - 2 + core
+        return pltpu.make_async_remote_copy(
+            src_ref=held.at[boundary, piece],
+            dst_ref=buf.at[array, place, :, cols(c)],
+            send_sem=hsend.at[boundary, piece],
+            recv_sem=recv_sem.at[place, array * CHUNKS + c],
+            device_id=device(target),
+            device_id_type=MESH,
+        )
+
+    def relay(array, c):
+        if (array, c) not in RELAYED:
+            return
+        piece = RELAYED.index((array, c))
+        for place, at in ((LOW, up_relay), (HIGH, down_relay)):
+
+            @pl.when(me == at)
+            def _():
+                for boundary in range(groups - 1):
+                    onward = from_relay(array, c, place, boundary)
+                    pltpu.make_async_copy(
+                        held.at[boundary, piece], held.at[boundary, piece], hrecv.at[boundary, piece]
+                    ).wait()
+                    onward.start()
+
+    def relay_sent():
+        for place, at in ((LOW, up_relay), (HIGH, down_relay)):
+
+            @pl.when(me == at)
+            def _():
+                for array, c in RELAYED:
+                    for boundary in range(groups - 1):
+                        from_relay(array, c, place, boundary).wait_send()
+
+    def start_own(array, c):
+        if (array, c) in RELAYED:
+            for place, crossing, present in ((LOW, closes, has_high), (HIGH, opens, has_low)):
+                where(crossing, lambda: to_relay(array, c, place).start())
+                where(present & jnp.logical_not(crossing), lambda: step(array, c, place).start())
+        else:
+            start(array, c, LOW)
+            start(array, c, HIGH)
+        start(array, c, MATE)
+
     def forward(array, c):
-        r = routes(array, c)
-        r[LOW].wait_recv()
-
-        @pl.when(core == 1)
-        def _():
-            far_copy(array, c, LOW).start()
-
-        r[MATE_LOW].start()
-        r[HIGH].wait_recv()
-
-        @pl.when(core == 0)
-        def _():
-            far_copy(array, c, HIGH).start()
-
-        r[MATE_HIGH].start()
+        relay(array, c)
+        for place, onward, owner in ((LOW, MATE_LOW, 1), (HIGH, MATE_HIGH, 0)):
+            wait_recv(array, c, place)
+            where(gives_far & (core == owner), lambda: far_copy(array, c, place).start())
+            start(array, c, onward)
 
     def wait_gathered(array, c):
-        r = routes(array, c)
-        r[MATE].wait_recv()
-        r[MATE_LOW].wait_recv()
-        r[MATE_HIGH].wait_recv()
-        far_copy(array, c, LOW).wait_recv()
+        for place in (MATE, MATE_LOW, MATE_HIGH):
+            wait_recv(array, c, place)
+        where(has_far, lambda: far_copy(array, c, LOW).wait_recv())
 
     def wait_sent(array, c):
-        r = routes(array, c)
-        for place in (LOW, HIGH, MATE, MATE_LOW, MATE_HIGH):
-            r[place].wait_send()
-        far_copy(array, c, LOW).wait_send()
+        for place in steps:
+            where(steps[place][2], lambda: step(array, c, place).wait_send())
+        where(gives_far, lambda: far_copy(array, c, LOW).wait_send())
 
     locals_ = [pltpu.make_async_copy(refs[a], buf.at[a, OWN], loc_sem.at[a]) for a in range(4)]
     for copy in locals_:
@@ -114,9 +181,21 @@
     barrier = pltpu.get_barrier_semaphore()
     for distance in (-3, -2, -1, 1, 2, 3):
         pl.semaphore_signal(barrier, inc=1, device_id=device(me + distance), device_id_type=MESH)
-    pl.semaphore_wait(barrier, 6)
-
-    order = [(K, c) for c in range(0)]
+    for condition, partners in (
+        (opens | closes, [first, last]),
+        ((me == first) | (me == last),
+         [b * inner + inner - 2 + core for b in range(groups - 1)] + [(b + 1) * inner + core for b in range(groups - 1)]),
+    ):
+
+        @pl.when(condition)
+        def _():
+            for partner in partners:
+                pl.semaphore_signal(barrier, inc=1, device_id=device(partner), device_id_type=MESH)
+
+    expected = 6 + jnp.where(opens | closes, 2, 0) + jnp.where((me == first) | (me == last), 2 * (groups - 1), 0)
+    pl.semaphore_wait(barrier, expected)
+
+    order = []
     for c in range(CHUNKS):
         order += [(K, c), (V, c)]
     for c in range(CHUNKS):
@@ -139,6 +218,16 @@
     inside = (across >= 0) & (across < devices * rows)
     seg_across = jnp.where(inside, seg_across, -1)
     bias[...] = jnp.where(seg_down == seg_across, 0.0, NEG)
+
+    def clear(place):
+        def body(array, carry):
+            buf[array, place] = jnp.zeros((rows, width), jnp.bfloat16)
+            return carry
+
+        lax.fori_loop(0, 4, body, 0)
+
+    for place, present in ((LOW, has_low), (MATE_LOW, has_low), (HIGH, has_high), (MATE_HIGH, has_high), (FAR, has_far)):
+        pl.when(jnp.logical_not(present))(functools.partial(clear, place))
 
     for copy in locals_:
         copy.wait()
@@ -224,6 +313,7 @@
 
     for array, c in order:
         wait_sent(array, c)
+    relay_sent()
     for copy in stat_copies:
         copy.wait_send()
 
@@ -246,11 +336,14 @@
                 pltpu.VMEM((4, 7, rows, width), jnp.bfloat16),
                 pltpu.VMEM((rows, 7 * rows), jnp.float32),
                 pltpu.VMEM((7, 2, stat_rows, rows), jnp.float32),
+                pltpu.VMEM((groups - 1, len(RELAYED), rows, (heads // CHUNKS) * HEAD_DIM), jnp.bfloat16),
                 pltpu.SemaphoreType.DMA((7, pieces)),
                 pltpu.SemaphoreType.DMA((7, pieces)),
                 pltpu.SemaphoreType.DMA((4,)),
                 pltpu.SemaphoreType.DMA((7,)),
                 pltpu.SemaphoreType.DMA((7,)),
+                pltpu.SemaphoreType.DMA((groups - 1, len(RELAYED))),
+                pltpu.SemaphoreType.DMA((groups - 1, len(RELAYED))),
             ],
             compiler_params=pltpu.CompilerParams(
                 collective_id=0, has_side_effects=True, vmem_limit_bytes=48 * 1024 * 1024

time: 148 us -> 141 us (0.953); the launches traced: 145 us -> 140 us
  Pallas kernels: 137 us -> 133 us
    pallas_call x1, Pallas kernels: 137 us -> 133 us  [on_device(): pl.pallas_call(functools.partial(kernel, groups, inner), out_shape=(block...]
where the time goes in v2:
time: 141 us; the launch traced here: 140 us
  Pallas kernels  133 us (94%)
  local copies, waits for them, and re-layouts  7.02 us (5%)
    pallas_call x1, Pallas kernels, on_device(): pl.pallas_call(functools.partial(kernel, groups, inner), out_shape=(block...  133 us
    unnamed x13, local copies, waits for them, and re-layouts  7.02 us

profile of v2, /device:TPU:29, one launch (start us, length us, event | category | flops | bytes accessed | tf_op | source)
XLA Modules:
  0.0 140.3 jit_solution(14823244426532158378)
XLA Ops:
  0.6 0.0 copy-start
  0.6 1.0 copy-done
  1.7 0.0 copy-start.1
  1.7 1.0 copy-done.1
  2.7 0.0 copy-start.2
  2.7 1.0 copy-done.2
  3.7 0.0 copy-start.3
  3.7 1.0 copy-done.3
  4.7 0.0 copy-start.4
  4.7 0.7 copy-done.4
  5.4 132.6 %shard_map.76 = (bf16[128,1792]{1,0:T(8,128)(2,1)S(1)}, bf16[128,1792]{1,0:T(8,128)(2,1)S(1)}, bf16[128,1792]{1,0:T(8,128)(2,1)S(1)}) custom-call(bf16[128,1792]{1,0:T(8,128)(2,1)S(1)} %copy-done, bf16[128,1792]{1,0:T(8,128)(2,1)S(1)} %copy-done.1, bf16[128,1792]{1,0:T(8,128)(2,1)S(1)} %copy-done.2, bf16[128,1792]{1,0:T(8,128)(2,1)S(1)} %copy-done.3, ...), custom_call_target="tpu_custom_call" | custom-call | tf_op jit(solution)/shard_map/pallas_call | solution.py:330
  138.0 0.8 copy.11
  138.7 0.8 copy.12
  139.5 0.8 copy.13
Async XLA Ops:
  0.6 1.0 copy-start
  1.7 1.0 copy-start.1
  2.7 1.0 copy-start.2
  3.7 1.0 copy-start.3
  4.7 0.7 copy-start.4

commit v3 on v2

--- a/solution.py
+++ b/solution.py
@@ -265,6 +265,9 @@
         wait_gathered(K, c)
         wait_gathered(V, c)
         totals = lax.fori_loop(c * per, (c + 1) * per, first_pass, totals)
+        if c < CHUNKS - 1:
+            forward(Q, c)
+            forward(G, c)
     stat[0, 0] = totals[0].T[:stat_rows]
     stat[0, 1] = totals[1].T[:stat_rows]
 
@@ -285,9 +288,8 @@
     for copy in stat_copies:
         copy.start()
 
-    for c in range(CHUNKS):
-        forward(Q, c)
-        forward(G, c)
+    forward(Q, CHUNKS - 1)
+    forward(G, CHUNKS - 1)
     for copy in stat_copies:
         copy.wait_recv()
 

time: 141 us -> 135 us (0.957)
  Pallas kernels: 133 us -> 126 us
    pallas_call x1, Pallas kernels: 133 us -> 126 us  [on_device(): pl.pallas_call(functools.partial(kernel, groups, inner), out_shape=(block...]
where the time goes in v3:
time: 135 us; the launch traced here: 134 us
  Pallas kernels  126 us (93%)
  local copies, waits for them, and re-layouts  7.02 us (5%)
    pallas_call x1, Pallas kernels, on_device(): pl.pallas_call(functools.partial(kernel, groups, inner), out_shape=(block...  126 us
    unnamed x13, local copies, waits for them, and re-layouts  7.02 us

profile of v3, /device:TPU:29, one launch (start us, length us, event | category | flops | bytes accessed | tf_op | source)
XLA Modules:
  0.0 134.2 jit_solution(18334250259532082043)
XLA Ops:
  0.6 0.0 copy-start
  0.6 1.0 copy-done
  1.7 0.0 copy-start.1
  1.7 1.0 copy-done.1
  2.7 0.0 copy-start.2
  2.7 1.0 copy-done.2
  3.7 0.0 copy-start.3
  3.7 1.0 copy-done.3
  4.7 0.0 copy-start.4
  4.7 0.7 copy-done.4
  5.4 126.5 %shard_map.76 = (bf16[128,1792]{1,0:T(8,128)(2,1)S(1)}, bf16[128,1792]{1,0:T(8,128)(2,1)S(1)}, bf16[128,1792]{1,0:T(8,128)(2,1)S(1)}) custom-call(bf16[128,1792]{1,0:T(8,128)(2,1)S(1)} %copy-done, bf16[128,1792]{1,0:T(8,128)(2,1)S(1)} %copy-done.1, bf16[128,1792]{1,0:T(8,128)(2,1)S(1)} %copy-done.2, bf16[128,1792]{1,0:T(8,128)(2,1)S(1)} %copy-done.3, ...), custom_call_target="tpu_custom_call" | custom-call | tf_op jit(solution)/shard_map/pallas_call | solution.py:332
  131.9 0.8 copy.11
  132.6 0.8 copy.12
  133.4 0.8 copy.13
Async XLA Ops:
  0.6 1.0 copy-start
  1.7 1.0 copy-start.1
  2.7 1.0 copy-start.2
  3.7 1.0 copy-start.3
  4.7 0.7 copy-start.4
